TPU v7x, 32 devices: a whole 2x2x4 slice. The times are simulated.
32 devices in a mesh: ctx: 8 (over z, y), tp: 4 (over x, core).
Axes of the slice: x: 2, y: 2, z: 4, core: 2. Of those that a mesh axis runs over, the one named last changes fastest.
Arguments:
- query_proj: bfloat16 [1024, 4096], P('ctx', 'tp'), may hold values from -6 to 6
- key_proj: bfloat16 [1024, 4096], P('ctx', 'tp'), may hold values from -6 to 6
- value_proj: bfloat16 [1024, 4096], P('ctx', 'tp'), may hold values from -6 to 6
- filters: float32 [256, 128], P('tp'), may hold values from -0.5 to 0.5
- skip_gain: float32 [4096], P('tp'), may hold values from -1 to 1
- out_grad: bfloat16 [1024, 4096], P('ctx', 'tp'), may hold values from -6 to 6
- w_out: bfloat16 [4096, 4096], P('tp'), may hold values from -0.09375 to 0.09375
Outputs:
- query_grad: bfloat16 [1024, 4096], P('ctx', 'tp')
- key_grad: bfloat16 [1024, 4096], P('ctx', 'tp')
- value_grad: bfloat16 [1024, 4096], P('ctx', 'tp')
- filter_grad: float32 [256, 128], P('tp')
- skip_grad: float32 [4096], P('tp')
All inputs are finite; a program needn't handle non-finite values.
Results may differ from a plain program's by a relative error of at most 0.0075.
Values may be sent and summed in bfloat16 or wider, within the bound.
A program may use at most 128 MiB of HBM per device.

v0:
```python
import jax
import jax.numpy as jnp
from jax import lax
from jax.sharding import PartitionSpec as P


def passed_along(block, axis, distance):
    devices = range(lax.axis_size(axis))
    route = [(i - distance, i) for i in devices if i - distance in devices]
    return lax.ppermute(block, axis, route)


def blocks_of(extended, width):
    count = (extended.shape[0] - width) // width
    channels = extended.shape[1]
    first = extended[:-width].reshape(count, width, channels)
    second = extended[width:].reshape(count, width, channels)
    return jnp.concatenate([first, second], axis=1)


def tap_table(filters, causal):
    width = filters.shape[1]
    rows = jnp.arange(width)[:, None]
    cols = jnp.arange(2 * width)[None, :]
    lag = rows + width - cols if causal else cols - rows
    valid = (lag >= 0) & (lag < width)
    index = jnp.clip(lag, 0, width - 1)
    table = filters[:, index]
    return jnp.where(valid[None], table, jnp.float32(0.0))


def convolve(extended, filters, skip_gain, causal):
    width = filters.shape[1]
    groups = filters.shape[0]
    channels = extended.shape[1]
    window = blocks_of(extended, width)
    count = window.shape[0]
    window = window.reshape(count, 2 * width, groups, channels // groups).astype(jnp.float32)
    mixed = jnp.einsum(
        "gij,bjgc->bigc", tap_table(filters, causal), window, precision=lax.Precision.HIGHEST
    )
    mixed = mixed.reshape(count * width, channels)
    current = extended[width:] if causal else extended[:-width]
    return mixed + skip_gain[None, :] * current.astype(jnp.float32)


def diagonal_lags(pairs, width):
    leading = pairs.shape[:-2]
    flat = pairs.reshape(leading + (width * 2 * width,))
    padded = jnp.concatenate([flat, jnp.zeros(leading + (width,), jnp.float32)], axis=-1)
    skewed = padded.reshape(leading + (width, 2 * width + 1)).sum(axis=-2)
    return skewed[..., width:0:-1]


def on_device(query_proj, key_proj, value_proj, filters, skip_gain, out_grad, w_out):
    width = filters.shape[1]
    groups = filters.shape[0]
    tok_rows = query_proj.shape[0]
    channels = query_proj.shape[1]
    span = channels // groups
    rim_rows = width - 1
    count = tok_rows // width
    query_f = query_proj.astype(jnp.float32)
    key_f = key_proj.astype(jnp.float32)
    value_f = value_proj.astype(jnp.float32)
    products = (key_f * value_f).astype(jnp.bfloat16)
    product_f = products.astype(jnp.float32)
    mixer_grad = lax.dot_general(
        lax.all_gather(out_grad, "tp", axis=1, tiled=True),
        w_out,
        (((1,), (1,)), ((), ())),
        preferred_element_type=jnp.float32,
    )
    earlier = passed_along(products[tok_rows - rim_rows :], "ctx", 1)
    single = jnp.zeros((1, channels), jnp.bfloat16)
    prod_ext = jnp.concatenate([single, earlier, products], axis=0)
    filtered = convolve(prod_ext, filters, skip_gain, True)
    query_grad = (mixer_grad * filtered).astype(jnp.bfloat16)
    filtered_grad = (mixer_grad * query_f).astype(jnp.bfloat16)
    grad_f = filtered_grad.astype(jnp.float32)
    later = passed_along(filtered_grad[:rim_rows], "ctx", -1)
    grad_ext = jnp.concatenate([filtered_grad, later, single], axis=0)
    product_grad = convolve(grad_ext, filters, skip_gain, False)
    key_grad = (product_grad * value_f).astype(jnp.bfloat16)
    value_grad = (product_grad * key_f).astype(jnp.bfloat16)
    window = blocks_of(prod_ext, width)
    grad_blocks = filtered_grad.reshape(count, width, channels)
    skip_part = jnp.sum(grad_f * product_f, axis=0)
    pairs = jnp.einsum(
        "bigc,bjgc->gij",
        grad_blocks.reshape(count, width, groups, span),
        window.reshape(count, 2 * width, groups, span),
        preferred_element_type=jnp.float32,
    )
    grouped = diagonal_lags(pairs, width)
    filter_grad, skip_grad = lax.psum((grouped, skip_part), "ctx")
    return (query_grad, key_grad, value_grad, filter_grad, skip_grad)


def solution(mesh):
    return jax.shard_map(
        on_device,
        mesh=mesh,
        in_specs=(
            P("ctx", "tp"),
            P("ctx", "tp"),
            P("ctx", "tp"),
            P("tp", None),
            P("tp"),
            P("ctx", "tp"),
            P("tp", None),
        ),
        out_specs=(P("ctx", "tp"), P("ctx", "tp"), P("ctx", "tp"), P("tp", None), P("tp")),
        check_vma=False,
    )
```

profile of v0, /device:TPU:0, one launch (start us, length us, event | category | flops | bytes accessed | tf_op | source)
XLA Modules:
  0.0 376.2 jit_solution(13880040861033989793)
XLA Ops:
  7.2 0.7 all-gather.2.cloned.1.call-update
  8.0 0.1 copy.37
  8.0 0.1 fusion.21
  8.1 0.1 copy.36
  8.3 20.7 %all-gather.2.cloned.1.call-done = bf16[128,4096]{1,0:T(8,128)(2,1)} async-done(((bf16[128,1024]{1,0:T(8,128)(2,1)}), bf16[128,4096]{1,0:T(8,128)(2,1)}) %all-gather.2.cloned.1.call-update) | async-done | bytes 1048592 | tf_op jit(solution)/shard_map/all_gather | solution.py:69
  29.0 6.7 %fusion.17 = (f32[1024]{0:T(1024)S(1)}, bf16[128,1024]{1,0:T(8,128)(2,1)S(1)}, bf16[128,1024]{1,0:T(8,128)(2,1)S(1)}, f32[128,1024]{1,0:T(8,128)S(1)}) fusion(bf16[128,1024]{1,0:T(8,128)(2,1)} %param.7, bf16[128,1024]{1,0:T(8,128)(2,1)} %param.9, bf16[128,1024]{1,0:T(8,128)(2,1)} %param.8, bf16[128,4096]{1,0:T(8,128)(2,1)} %all-gather.2.cloned.1.call-done, ...), kind=kOutput, calls=%fused_computation.25 | convolution fusion | flops 1075182592 | bytes 11276288 | tf_op jit(solution)/shard_map/dot_general | solution.py:68
  35.8 1.3 collective-permute-start.1
  37.1 0.1 copy.25
  37.2 108.4 %gather_fusion.1 = f32[32768,64]{1,0:T(8,128)} fusion(f32[64,128]{0,1:T(8,128)S(1)} %copy.25, s32[32768]{0:T(1024)S(1)} %broadcast_clamp_fusion), kind=kCustom, calls=%fused_computation.1 | custom fusion | bytes 16908288 | tf_op jit(solution)/shard_map/gather | solution.py:28
  145.6 13.6 %copy.31 = f32[128,256,64]{1,0,2:T(8,128)} copy(f32[128,256,64]{2,1,0:T(8,128)} %bitcast.45) | data formatting | bytes 16777216 | tf_op jit(solution)/shard_map/gather | solution.py:28
  159.2 108.3 %gather_fusion = f32[32768,64]{1,0:T(8,128)} fusion(f32[64,128]{0,1:T(8,128)S(1)} %copy.25, s32[32768]{0:T(1024)S(1)} %broadcast_clamp_fusion.1), kind=kCustom, calls=%fused_computation | custom fusion | bytes 16908288 | tf_op jit(solution)/shard_map/gather | solution.py:28
  267.5 13.6 %copy.26 = f32[128,256,64]{1,0,2:T(8,128)} copy(f32[128,256,64]{2,1,0:T(8,128)} %bitcast.44) | data formatting | bytes 16777216 | tf_op jit(solution)/shard_map/gather | solution.py:28
  281.1 0.1 fusion.27
  281.2 0.2 copy.28
  281.4 0.2 copy.24
  281.6 4.7 %collective-permute-start = (bf16[127,1024]{1,0:T(8,128)(2,1)S(1)}, bf16[127,1024]{1,0:T(8,128)(2,1)S(1)}, u32[]{:S(2)}, u32[]{:S(2)}) collective-permute-start(bf16[127,1024]{1,0:T(8,128)(2,1)S(1)} %slice.19), channel_id=1, source_target_pairs={{0,4},{4,8},{8,12},{12,16},{16,20},{20,24},{24,28},{1,5},{5,9},{9,... | collective-permute-start | bytes 780296 | tf_op jit(solution)/shard_map/ppermute | solution.py:10
  286.4 0.2 copy.35
  286.6 6.5 %fusion = f32[64,16,128]{2,1,0:T(8,128)S(1)} fusion(f32[128,256,64]{1,0,2:T(8,128)} %copy.31, pred[128,256]{1,0:T(8,128)(4,1)S(1)} %fusion.28, bf16[1,128,64,16]{1,3,2,0:T(8,128)(2,1)S(1)} %bitcast.57, bf16[1,128,64,16]{1,3,2,0:T(8,128)(2,1)S(1)} %bitcast.50), kind=kOutput, calls=%fused_computation.2 | convolution fusion | flops 405798912 | bytes 9469952 | tf_op jit(solution)/shard_map/gij,bjgc->bigc/dot_general | solution.py:39
  293.2 0.2 copy.32
  293.4 0.2 copy.34
  293.6 0.1 concatenate.27.clone
  293.7 6.5 %fusion.2 = f32[64,16,128]{2,1,0:T(8,128)S(1)} fusion(f32[128,256,64]{1,0,2:T(8,128)} %copy.26, pred[128,256]{1,0:T(8,128)(4,1)S(1)} %fusion.27, bf16[1,128,64,16]{1,3,2,0:T(8,128)(2,1)S(1)} %bitcast.52, bf16[1,128,64,16]{1,3,2,0:T(8,128)(2,1)S(1)} %bitcast.48), kind=kOutput, calls=%fused_computation.4 | convolution fusion | flops 405798912 | bytes 9469952 | tf_op jit(solution)/shard_map/gij,bjgc->bigc/dot_general | solution.py:39
  300.3 0.2 copy.27
  300.5 1.3 fusion.20
  301.8 4.7 %copy.38 = f32[8,8,128,256]{3,1,2,0:T(8,128)S(1)} copy(f32[8,8,128,256]{3,2,1,0:T(8,128)S(1)} %bitcast.47) | data formatting | bytes 16777216
  306.5 3.8 concatenate.35
  310.3 14.2 %reshape.171 = f32[64,128,257]{2,1,0:T(8,128)} reshape(f32[64,32896]{1,0:T(8,128)} %concatenate.35) | data formatting | bytes 16842752 | tf_op jit(solution)/shard_map/reshape | solution.py:51
  324.4 6.1 %reduce_sum.18 = f32[64,257]{1,0:T(8,128)S(1)} reduce(f32[64,128,257]{2,1,0:T(8,128)} %reshape.171, f32[]{:T(128)} %constant.1.clone.1), dimensions={1}, to_apply=%region_0.1 | reduce | flops 2088896 | bytes 8487172 | tf_op jit(solution)/shard_map/reduce_sum | solution.py:51
  330.6 0.1 slice.21
  330.7 0.1 rev.3
  330.7 37.5 %all-reduce.3 = (f32[64,128]{1,0:T(8,128)}, f32[1024]{0:T(1024)}) all-reduce(f32[64,128]{1,0:T(8,128)S(1)} %rev.3, f32[1024]{0:T(1024)S(1)} %get-tuple-element.7), channel_id=1, replica_groups=mesh['ctx'=8,'tp'=4] {'ctx'}, use_global_device_ids=true, to_apply=%region_1.2 | all-reduce | flops 9216 | bytes 73728 | tf_op jit(solution)/shard_map/psum | solution.py:96
  368.3 1.1 fusion.10
  (18 shorter events, 0.3 us)
Async XLA Ops:
  7.2 29.9 %copy-start.2 = (f32[64,128]{1,0:T(8,128)S(1)}, f32[64,128]{1,0:T(8,128)}, u32[]{:S(2)}) copy-start(f32[64,128]{1,0:T(8,128)} %param.10) | copy-start | bytes 98308
  7.2 21.9 %all-gather.2.cloned.1.call-start = ((), (), s32[]{:S(2)}) async-start(), calls=%async_computation | async-start | bytes 1310720 | tf_op jit(solution)/shard_map/all_gather | solution.py:69
  35.8 250.6 %collective-permute-start.1 = (bf16[127,1024]{1,0:T(8,128)(2,1)S(1)}, bf16[127,1024]{1,0:T(8,128)(2,1)S(1)}, u32[]{:S(2)}, u32[]{:S(2)}) collective-permute-start(bf16[127,1024]{1,0:T(8,128)(2,1)S(1)} %bitcast.54), channel_id=1, source_target_pairs={{4,0},{8,4},{12,8},{16,12},{20,16},{24,20},{28,24},{5,1},{9,5},{13... | collective-permute-start | bytes 780296 | tf_op jit(solution)/shard_map/ppermute | solution.py:10
  281.6 11.8 %collective-permute-start = (bf16[127,1024]{1,0:T(8,128)(2,1)S(1)}, bf16[127,1024]{1,0:T(8,128)(2,1)S(1)}, u32[]{:S(2)}, u32[]{:S(2)}) collective-permute-start(bf16[127,1024]{1,0:T(8,128)(2,1)S(1)} %slice.19), channel_id=1, source_target_pairs={{0,4},{4,8},{8,12},{12,16},{16,20},{20,24},{24,28},{1,5},{5,9},{9,... | collective-permute-start | bytes 780296 | tf_op jit(solution)/shard_map/ppermute | solution.py:10
  324.4 43.8 %copy-start = (bf16[128,1024]{1,0:T(8,128)(2,1)S(1)}, bf16[128,1024]{1,0:T(8,128)(2,1)}, u32[]{:S(2)}) copy-start(bf16[128,1024]{1,0:T(8,128)(2,1)} %param.8) | copy-start | bytes 786436
  324.4 43.8 %copy-start.1 = (bf16[128,1024]{1,0:T(8,128)(2,1)S(1)}, bf16[128,1024]{1,0:T(8,128)(2,1)}, u32[]{:S(2)}) copy-start(bf16[128,1024]{1,0:T(8,128)(2,1)} %param.9) | copy-start | bytes 786436
  324.4 43.8 %copy-start.3 = (f32[1024]{0:T(1024)S(1)}, f32[1024]{0:T(1024)}, u32[]{:S(2)}) copy-start(f32[1024]{0:T(1024)} %param.11) | copy-start | bytes 12292
Sparse Core Ops, SparseCore 0:
  9.6 19.4 all-gather.1
where the time goes:
time: 377 us; the launch traced here: 376 us
  local copies, waits for them, and re-layouts  268 us (71%)
  blocking collectives  37.5 us (10%)
  waiting for transfers between devices  21.4 us (6%)
  matrix products  21.1 us (6%)
  between operations  14.2 us (4%)
  other arithmetic  7.52 us (2%)
  starting transfers between devices  6.07 us (2%)
    gather x4, local copies, waits for them, and re-layouts, tap_table(): table = filters[:, index]  244 us
    psum x1, blocking collectives, on_device(): filter_grad, skip_grad = lax.psum((grouped, skip_part), 'ctx')  37.5 us
    all_gather x1, waiting for transfers between devices, on_device(): lax.all_gather(out_grad, 'tp', axis=1, tiled=True)  20.7 us
    reshape x1, local copies, waits for them, and re-layouts, diagonal_lags(): skewed = padded.reshape(leading + (width, 2 * width + 1)).sum(axis=-2)  14.2 us
    dot_general x2, matrix products, convolve(): jnp.einsum('gij,bjgc->bigc', tap_table(filters, causal), window, precisio...  13.1 us
  transfers between devices with their start and end apart: 3, of which 1 were waited for; matrix products, arithmetic and copies ran while one was open for 67% of the time, Pallas kernels for 0%

commit v1 on v0

v1 whole, which is shorter than its diff:
```python
import functools

import jax
import jax.numpy as jnp
from jax import lax
from jax.experimental import pallas as pl
from jax.experimental.pallas import tpu as pltpu
from jax.sharding import PartitionSpec as P

MESH = pl.DeviceIdType.MESH
LANES = 128
NT = (((1,), (1,)), ((), ()))
PIECES = 2


def kernel(
    n_ctx, n_tp,
    q_ref, k_ref, v_ref, f_ref, s_ref, og_ref, w_hbm,
    qg_ref, kg_ref, vg_ref, fg_ref, sg_ref,
    wv, ogb, x, xp, g, gn, a1, b1, a2, b2, mg, filt, part, rsb, red,
    w_sem, og_send, og_recv, fw_send, x_send, x_recv, g_send, g_recv,
    rs_send, rs_recv, ag_send, ag_recv,
):
    rows, channels = q_ref.shape
    tiles = channels // LANES
    per_tile = f_ref.shape[0] // tiles
    span = LANES // per_tile
    wide = channels // PIECES
    step = n_ctx // tiles
    me = lax.axis_index("ctx")
    tp = lax.axis_index("tp")
    mate = tp + 1 - 2 * lax.rem(tp, 2)
    across = [lax.rem(tp + 2 * d, n_tp) for d in range(1, n_tp // 2)]
    across_mate = [a + 1 - 2 * lax.rem(a, 2) for a in across]
    order = [tp, mate] + across + across_mate

    w_copies = []
    for n, slot in enumerate(order):
        copy = pltpu.make_async_copy(
            w_hbm.at[:, pl.ds(pl.multiple_of(slot * channels, channels), channels)], wv.at[n], w_sem.at[n]
        )
        copy.start()
        w_copies.append(copy)

    barrier = pltpu.get_barrier_semaphore()
    for peer in order[1:]:
        pl.semaphore_signal(barrier, inc=1, device_id=(me, peer), device_id_type=MESH)

    @pl.loop(1, n_ctx)
    def _(d):
        pl.semaphore_signal(barrier, inc=1, device_id=(lax.rem(me + d, n_ctx), tp), device_id_type=MESH)

    @pl.loop(0, tiles)
    def _(i):
        cols = pl.ds(pl.multiple_of(i * LANES, LANES), LANES)
        x[i] = (k_ref[:, cols].astype(jnp.float32) * v_ref[:, cols].astype(jnp.float32)).astype(jnp.bfloat16)

    pl.semaphore_wait(barrier, n_tp - 1 + n_ctx - 1)

    def og_copy(p, n, peer):
        return pltpu.make_async_remote_copy(
            src_ref=og_ref.at[:, pl.ds(p * wide, wide)], dst_ref=ogb.at[tp, p],
            send_sem=og_send.at[n, p], recv_sem=og_recv.at[tp, p],
            device_id=(me, peer), device_id_type=MESH,
        )

    def forward_copy(slot, p, n):
        return pltpu.make_async_remote_copy(
            src_ref=ogb.at[slot, p], dst_ref=ogb.at[slot, p],
            send_sem=fw_send.at[n, p], recv_sem=og_recv.at[slot, p],
            device_id=(me, mate), device_id_type=MESH,
        )

    direct = across + [mate]
    for p in range(PIECES):
        for n, peer in enumerate(direct):
            og_copy(p, n, peer).start()

    x_copy = pltpu.make_async_remote_copy(
        src_ref=x, dst_ref=xp, send_sem=x_send, recv_sem=x_recv,
        device_id=(lax.rem(me + 1, n_ctx), tp), device_id_type=MESH,
    )

    @pl.when(me < n_ctx - 1)
    def _():
        x_copy.start()

    row = lax.broadcasted_iota(jnp.int32, (rows, LANES), 0)
    col = lax.broadcasted_iota(jnp.int32, (rows, LANES), 1)
    mirror = jnp.where(lax.rem(row + col, LANES) == 0, 1.0, 0.0).astype(jnp.bfloat16)

    def spread(line):
        return pltpu.roll(jnp.broadcast_to(line, (rows, LANES)), 0, 1, stride=1, stride_axis=0)

    @pl.loop(0, tiles)
    def _(i):
        taps = f_ref[pl.ds(pl.multiple_of(i * per_tile, per_tile), per_tile), :]
        back = jnp.dot(taps.astype(jnp.bfloat16), mirror, preferred_element_type=jnp.float32)
        for j in range(per_tile):
            at = pl.ds(j * LANES, LANES)
            c1 = spread(back[j : j + 1])
            a1[i, :, at] = jnp.where(col > row, c1, 0.0).astype(jnp.bfloat16)
            b1[i, :, at] = jnp.where(col <= row, c1, 0.0).astype(jnp.bfloat16)
            c2 = spread(taps[j : j + 1])
            a2[i, :, at] = jnp.where(col < row, c2, 0.0).astype(jnp.bfloat16)
            b2[i, :, at] = jnp.where(col >= row, c2, 0.0).astype(jnp.bfloat16)

    lane = lax.broadcasted_iota(jnp.int32, (1, LANES), 1)
    masks = [
        jnp.where((lane >= j * span) & (lane < (j + 1) * span), 1.0, 0.0).astype(jnp.bfloat16)
        for j in range(per_tile)
    ]

    def by_group(block):
        return jnp.concatenate([block * m for m in masks], axis=0)

    def project(n, block_of, first):
        @pl.loop(0, tiles // 2)
        def _(i):
            chans = pl.ds(pl.multiple_of(i * 2 * LANES, 2 * LANES), 2 * LANES)
            total = None
            for p in range(PIECES):
                term = lax.dot_general(
                    block_of(p), wv[n, chans, pl.ds(p * wide, wide)], NT, preferred_element_type=jnp.float32
                )
                total = term if total is None else total + term
            if first:
                mg[:, chans] = total
            else:
                mg[:, chans] += total

    w_copies[0].wait()
    project(0, lambda p: og_ref[:, pl.ds(p * wide, wide)], True)

    for p in range(PIECES):
        forward_copy(mate, p, 0).wait_recv()
    w_copies[1].wait()
    project(1, lambda p: ogb[mate, p], False)

    @pl.when(me > 0)
    def _():
        x_copy.wait_recv()

    @pl.when(me == 0)
    def _():
        xp[...] = jnp.zeros_like(xp)

    for p in range(PIECES):
        for n, a in enumerate(across):
            forward_copy(a, p, n).wait_recv()
            forward_copy(a, p, n).start()

    @pl.loop(0, tiles)
    def _(i):
        cols = pl.ds(pl.multiple_of(i * LANES, LANES), LANES)
        y = jnp.dot(a1[i], by_group(xp[i]), preferred_element_type=jnp.float32)
        y += jnp.dot(b1[i], by_group(x[i]), preferred_element_type=jnp.float32)
        filt[:, cols] = y + s_ref[:, cols] * x[i].astype(jnp.float32)

    for n, a in enumerate(across):
        w_copies[2 + n].wait()
        project(2 + n, lambda p, a=a: ogb[a, p], False)
    for n, a in enumerate(across_mate):
        for p in range(PIECES):
            forward_copy(a, p, n).wait_recv()
        w_copies[2 + len(across) + n].wait()
        project(2 + len(across) + n, lambda p, a=a: ogb[a, p], False)

    def g_copy(i):
        return pltpu.make_async_remote_copy(
            src_ref=g.at[i], dst_ref=gn.at[i], send_sem=g_send.at[i], recv_sem=g_recv.at[i],
            device_id=(lax.rem(me + n_ctx - 1, n_ctx), tp), device_id_type=MESH,
        )

    @pl.loop(0, tiles)
    def _(i):
        cols = pl.ds(pl.multiple_of(i * LANES, LANES), LANES)
        m = mg[:, cols]
        g[i] = (m * q_ref[:, cols].astype(jnp.float32)).astype(jnp.bfloat16)

        @pl.when(me > 0)
        def _():
            g_copy(i).start()

        qg_ref[:, cols] = (m * filt[:, cols]).astype(jnp.bfloat16)

    flip = jnp.where(row + col == rows - 1, 1.0, 0.0).astype(jnp.bfloat16)

    def upside_down(block):
        return jnp.dot(flip, block, preferred_element_type=jnp.float32).astype(jnp.bfloat16)

    @pl.loop(0, tiles)
    def _(i):
        gt = g[i]
        far = lax.dot_general(by_group(upside_down(xp[i])), gt, NT, preferred_element_type=jnp.float32)
        near = lax.dot_general(by_group(upside_down(x[i])), gt, NT, preferred_element_type=jnp.float32)
        for j in range(per_tile):
            at = slice(j * rows, (j + 1) * rows)
            pairs = jnp.where(col + row >= rows - 1, near[at], far[at])
            turned = pltpu.roll(pairs, 0, 1, stride=1, stride_axis=0)
            part[i, pl.ds(j, 1), :] = jnp.sum(turned, axis=0, keepdims=True)
        part[i, pl.ds(0, per_tile), :] = pltpu.roll(part[i, pl.ds(0, per_tile), :], 1, 1)
        both = gt.astype(jnp.float32) * x[i].astype(jnp.float32)
        part[i, pl.ds(per_tile, 8), :] = jnp.sum(both.reshape(rows // 8, 8, LANES), axis=0)

    def rs_copy(i):
        return pltpu.make_async_remote_copy(
            src_ref=part.at[i], dst_ref=rsb.at[me], send_sem=rs_send.at[i], recv_sem=rs_recv.at[me],
            device_id=(i * step, tp), device_id_type=MESH,
        )

    def rs_arrival(d):
        source = lax.rem(me + d, n_ctx)
        return source, pltpu.make_async_remote_copy(
            src_ref=part.at[0], dst_ref=rsb.at[source], send_sem=rs_send.at[0], recv_sem=rs_recv.at[source],
            device_id=(source, tp), device_id_type=MESH,
        )

    mine = me // step
    owner = lax.rem(me, step) == 0

    @pl.loop(0, tiles)
    def _(i):
        @pl.when(i * step != me)
        def _():
            rs_copy(i).start()

    @pl.loop(0, tiles)
    def _(i):
        cols = pl.ds(pl.multiple_of(i * LANES, LANES), LANES)
        z = jnp.dot(b2[i], by_group(g[i]), preferred_element_type=jnp.float32)
        mg[:, cols] = z + s_ref[:, cols] * g[i].astype(jnp.float32)

    def ag_copy(d):
        return pltpu.make_async_remote_copy(
            src_ref=red.at[mine], dst_ref=red.at[mine], send_sem=ag_send.at[d], recv_sem=ag_recv.at[mine],
            device_id=(lax.rem(me + d, n_ctx), tp), device_id_type=MESH,
        )

    def ag_arrival(i):
        return pltpu.make_async_remote_copy(
            src_ref=red.at[i], dst_ref=red.at[i], send_sem=ag_send.at[0], recv_sem=ag_recv.at[i],
            device_id=(i * step, tp), device_id_type=MESH,
        )

    @pl.when(owner)
    def _():
        def gather(d, total):
            source, arrival = rs_arrival(d)
            arrival.wait_recv()
            return total + rsb[source]

        red[mine] = lax.fori_loop(1, n_ctx, gather, part[mine])

        @pl.loop(1, n_ctx)
        def _(d):
            ag_copy(d).start()

    @pl.loop(0, tiles)
    def _(i):
        cols = pl.ds(pl.multiple_of(i * LANES, LANES), LANES)

        @pl.when(me < n_ctx - 1)
        def _():
            g_copy(i).wait_recv()
            mg[:, cols] += jnp.dot(a2[i], by_group(gn[i]), preferred_element_type=jnp.float32)

        z = mg[:, cols]
        kg_ref[:, cols] = (z * v_ref[:, cols].astype(jnp.float32)).astype(jnp.bfloat16)
        vg_ref[:, cols] = (z * k_ref[:, cols].astype(jnp.float32)).astype(jnp.bfloat16)

    for i in range(tiles):
        @pl.when(i * step != me)
        def _():
            ag_arrival(i).wait_recv()

        fg_ref[pl.ds(i * per_tile, per_tile), :] = red[i, pl.ds(0, per_tile), :]
        sg_ref[:, pl.ds(i * LANES, LANES)] = jnp.sum(red[i, pl.ds(per_tile, 8), :], axis=0, keepdims=True)

    for p in range(PIECES):
        for n, peer in enumerate(direct):
            og_copy(p, n, peer).wait_send()
        for n, a in enumerate(across):
            forward_copy(a, p, n).wait_send()

    @pl.when(me < n_ctx - 1)
    def _():
        x_copy.wait_send()

    @pl.when(me > 0)
    def _():
        @pl.loop(0, tiles)
        def _(i):
            g_copy(i).wait_send()

    @pl.loop(0, tiles)
    def _(i):
        @pl.when(i * step != me)
        def _():
            rs_copy(i).wait_send()

    @pl.when(owner)
    def _():
        @pl.loop(1, n_ctx)
        def _(d):
            ag_copy(d).wait_send()


def on_device(n_ctx, n_tp, q, k, v, filters, skip_gain, out_grad, w_out):
    rows, channels = q.shape
    tiles = channels // LANES
    groups = filters.shape[0]
    block = (groups // tiles) + 8
    vmem = pl.BlockSpec(memory_space=pltpu.VMEM)
    bf, fl = jnp.bfloat16, jnp.float32
    dma = pltpu.SemaphoreType.DMA
    table = pltpu.VMEM((tiles, rows, (groups // tiles) * LANES), bf)
    slab = pltpu.VMEM((tiles, rows, LANES), bf)
    out = pl.pallas_call(
        functools.partial(kernel, n_ctx, n_tp),
        out_shape=(
            jax.ShapeDtypeStruct((rows, channels), bf),
            jax.ShapeDtypeStruct((rows, channels), bf),
            jax.ShapeDtypeStruct((rows, channels), bf),
            jax.ShapeDtypeStruct(filters.shape, fl),
            jax.ShapeDtypeStruct((1, channels), fl),
        ),
        in_specs=[vmem] * 6 + [pl.BlockSpec(memory_space=pl.ANY)],
        out_specs=(vmem,) * 5,
        scratch_shapes=[
            pltpu.VMEM((n_tp, channels, channels), bf),
            pltpu.VMEM((n_tp, PIECES, rows, channels // PIECES), bf),
            slab, slab, slab, slab,
            table, table, table, table,
            pltpu.VMEM((rows, channels), fl),
            pltpu.VMEM((rows, channels), fl),
            pltpu.VMEM((tiles, block, LANES), fl),
            pltpu.VMEM((n_ctx, block, LANES), fl),
            pltpu.VMEM((tiles, block, LANES), fl),
            dma((n_tp,)),
            dma((n_tp // 2, PIECES)),
            dma((n_tp, PIECES)),
            dma((n_tp // 2, PIECES)),
            dma, dma,
            dma((tiles,)), dma((tiles,)),
            dma((tiles,)), dma((n_ctx,)),
            dma((n_ctx,)), dma((tiles,)),
        ],
        compiler_params=pltpu.CompilerParams(
            collective_id=0, has_side_effects=True, vmem_limit_bytes=48 * 1024 * 1024
        ),
        cost_estimate=pl.CostEstimate(
            flops=2 * rows * channels * channels * n_tp, bytes_accessed=2 * channels * channels * n_tp, transcendentals=0
        ),
    )(q, k, v, filters, skip_gain.reshape(1, channels), out_grad, w_out)
    return out[:4] + (out[4].reshape(channels),)


def solution(mesh):
    n_ctx, n_tp = mesh.shape["ctx"], mesh.shape["tp"]
    return jax.shard_map(
        functools.partial(on_device, n_ctx, n_tp),
        mesh=mesh,
        in_specs=(
            P("ctx", "tp"),
            P("ctx", "tp"),
            P("ctx", "tp"),
            P("tp", None),
            P("tp"),
            P("ctx", "tp"),
            P("tp", None),
        ),
        out_specs=(P("ctx", "tp"), P("ctx", "tp"), P("ctx", "tp"), P("tp", None), P("tp")),
        check_vma=False,
    )
```

time: 377 us -> 42 us (0.11)
  local copies, waits for them, and re-layouts: 268 us -> 8.55 us
  blocking collectives: 37.5 us -> 0 us
  Pallas kernels: 0 us -> 32.5 us
  waiting for transfers between devices: 21.4 us -> 0 us
  matrix products: 21.1 us -> 0 us
  between operations: 14.2 us -> 0.66 us
  other arithmetic: 7.52 us -> 0 us
  starting transfers between devices: 6.07 us -> 0 us
    gather x4 -> x0, local copies, waits for them, and re-layouts: 244 us -> none  [tap_table(): table = filters[:, index]]
    psum x1 -> x0, blocking collectives: 37.5 us -> none  [on_device(): filter_grad, skip_grad = lax.psum((grouped, skip_part), 'ctx')]
    pallas_call x0 -> x1, Pallas kernels: none -> 32.5 us  [on_device(): pl.pallas_call(functools.partial(kernel, n_ctx, n_tp), out_shape=(jax.Sha...]
    dot_general x4 -> x0, matrix products: 21.1 us -> none  [the longest x2 13.1 us: convolve(): jnp.einsum('gij,bjgc->bigc', tap_table(filters, causal), window, precisio...]
    all_gather x1 -> x0, waiting for transfers between devices: 20.7 us -> none  [on_device(): lax.all_gather(out_grad, 'tp', axis=1, tiled=True)]
    reshape x3 -> x0, local copies, waits for them, and re-layouts: 14.6 us -> none  [the longest x1 14.2 us: diagonal_lags(): skewed = padded.reshape(leading + (width, 2 * width + 1)).sum(axis=-2)]
    reduce_sum x1 -> x0, other arithmetic: 6.14 us -> none  [diagonal_lags(): skewed = padded.reshape(leading + (width, 2 * width + 1)).sum(axis=-2)]
    ppermute x2 -> x0, starting transfers between devices: 6.03 us -> none  [passed_along(): return lax.ppermute(block, axis, route)]
  transfers between devices with their start and end apart: 3 -> 0, of which waited for: 1 -> 0; matrix products, arithmetic and copies ran while one was open for 67% -> 0% of each run, Pallas kernels for 0% -> 0%
where the time goes in v1:
time: 42 us; the launch traced here: 41.7 us
  Pallas kernels  32.5 us (77%)
  local copies, waits for them, and re-layouts  8.55 us (20%)
  between operations  0.66 us (2%)
    pallas_call x1, Pallas kernels, on_device(): pl.pallas_call(functools.partial(kernel, n_ctx, n_tp), out_shape=(jax.Sha...  32.5 us
    unnamed x17, local copies, waits for them, and re-layouts  8.55 us

profile of v1, /device:TPU:0, one launch (start us, length us, event | category | flops | bytes accessed | tf_op | source)
XLA Modules:
  0.0 41.7 jit_solution(672576066338805990)
XLA Ops:
  0.6 0.0 copy-start
  0.6 0.9 %copy-done = bf16[128,1024]{1,0:T(8,128)(2,1)S(1)} copy-done((bf16[128,1024]{1,0:T(8,128)(2,1)S(1)}, bf16[128,1024]{1,0:T(8,128)(2,1)}, u32[]{:S(2)}) %copy-start) | copy-done | bytes 262168
  1.6 0.0 copy-start.1
  1.6 0.9 %copy-done.1 = bf16[128,1024]{1,0:T(8,128)(2,1)S(1)} copy-done((bf16[128,1024]{1,0:T(8,128)(2,1)S(1)}, bf16[128,1024]{1,0:T(8,128)(2,1)}, u32[]{:S(2)}) %copy-start.1) | copy-done | bytes 262168
  2.5 0.0 copy-start.2
  2.5 0.9 %copy-done.2 = bf16[128,1024]{1,0:T(8,128)(2,1)S(1)} copy-done((bf16[128,1024]{1,0:T(8,128)(2,1)S(1)}, bf16[128,1024]{1,0:T(8,128)(2,1)}, u32[]{:S(2)}) %copy-start.2) | copy-done | bytes 262168
  3.5 0.0 copy-start.3
  3.5 0.9 %copy-done.3 = bf16[128,1024]{1,0:T(8,128)(2,1)S(1)} copy-done((bf16[128,1024]{1,0:T(8,128)(2,1)S(1)}, bf16[128,1024]{1,0:T(8,128)(2,1)}, u32[]{:S(2)}) %copy-start.3) | copy-done | bytes 262168
  4.4 0.0 copy-start.4
  4.4 0.8 %copy-done.4 = f32[64,128]{1,0:T(8,128)S(1)} copy-done((f32[64,128]{1,0:T(8,128)S(1)}, f32[64,128]{1,0:T(8,128)}, u32[]{:S(2)}) %copy-start.4) | copy-done | bytes 32792
  5.2 0.0 copy-start.5
  5.2 0.7 %copy-done.5 = f32[1024]{0:T(1024)S(1)} copy-done((f32[1024]{0:T(1024)S(1)}, f32[1024]{0:T(1024)}, u32[]{:S(2)}) %copy-start.5) | copy-done | bytes 4120
  5.9 32.5 %shard_map.110 = (bf16[128,1024]{1,0:T(8,128)(2,1)S(1)}, bf16[128,1024]{1,0:T(8,128)(2,1)S(1)}, bf16[128,1024]{1,0:T(8,128)(2,1)S(1)}, f32[64,128]{1,0:T(8,128)S(1)}, f32[1,1024]{1,0:T(1,128)S(1)}) custom-call(bf16[128,1024]{1,0:T(8,128)(2,1)S(1)} %copy-done, bf16[128,1024]{1,0:T(8,128)(2,1)S(1)} %copy-done.1, bf16[128,1024]{1,0:T(8,128)(2,1)S(1)} %copy-done.2, ...), custom_call_target="tpu_custom_call" | custom-call | flops 1073741824 | bytes 8388608 | tf_op jit(solution)/shard_map/pallas_call | solution.py:319
  38.4 0.7 %copy.17 = bf16[128,1024]{1,0:T(8,128)(2,1)} copy(bf16[128,1024]{1,0:T(8,128)(2,1)S(1)} %get-tuple-element.20) | data formatting | bytes 524288
  39.1 0.7 %copy.18 = bf16[128,1024]{1,0:T(8,128)(2,1)} copy(bf16[128,1024]{1,0:T(8,128)(2,1)S(1)} %get-tuple-element.21) | data formatting | bytes 524288
  39.8 0.7 %copy.19 = bf16[128,1024]{1,0:T(8,128)(2,1)} copy(bf16[128,1024]{1,0:T(8,128)(2,1)S(1)} %get-tuple-element.22) | data formatting | bytes 524288
  40.5 0.6 %copy.20 = f32[64,128]{1,0:T(8,128)} copy(f32[64,128]{1,0:T(8,128)S(1)} %get-tuple-element.23) | data formatting | bytes 65536
  41.1 0.6 %copy.21 = f32[1024]{0:T(1024)} copy(f32[1024]{0:T(1024)S(1)} %bitcast.3) | data formatting | bytes 8192
Async XLA Ops:
  0.6 1.0 %copy-start = (bf16[128,1024]{1,0:T(8,128)(2,1)S(1)}, bf16[128,1024]{1,0:T(8,128)(2,1)}, u32[]{:S(2)}) copy-start(bf16[128,1024]{1,0:T(8,128)(2,1)} %q_ref.1) | copy-start | bytes 786436
  1.6 0.9 %copy-start.1 = (bf16[128,1024]{1,0:T(8,128)(2,1)S(1)}, bf16[128,1024]{1,0:T(8,128)(2,1)}, u32[]{:S(2)}) copy-start(bf16[128,1024]{1,0:T(8,128)(2,1)} %k_ref.1) | copy-start | bytes 786436
  2.5 0.9 %copy-start.2 = (bf16[128,1024]{1,0:T(8,128)(2,1)S(1)}, bf16[128,1024]{1,0:T(8,128)(2,1)}, u32[]{:S(2)}) copy-start(bf16[128,1024]{1,0:T(8,128)(2,1)} %v_ref.1) | copy-start | bytes 786436
  3.5 0.9 %copy-start.3 = (bf16[128,1024]{1,0:T(8,128)(2,1)S(1)}, bf16[128,1024]{1,0:T(8,128)(2,1)}, u32[]{:S(2)}) copy-start(bf16[128,1024]{1,0:T(8,128)(2,1)} %og_ref.1) | copy-start | bytes 786436
  4.4 0.8 %copy-start.4 = (f32[64,128]{1,0:T(8,128)S(1)}, f32[64,128]{1,0:T(8,128)}, u32[]{:S(2)}) copy-start(f32[64,128]{1,0:T(8,128)} %f_ref.1) | copy-start | bytes 98308
  5.2 0.7 %copy-start.5 = (f32[1024]{0:T(1024)S(1)}, f32[1024]{0:T(1024)}, u32[]{:S(2)}) copy-start(f32[1024]{0:T(1024)} %param.11) | copy-start | bytes 12292

commit v2 on v1

--- a/solution.py
+++ b/solution.py
@@ -15,8 +15,9 @@
 
 def kernel(
     n_ctx, n_tp,
-    q_ref, k_ref, v_ref, f_ref, s_ref, og_ref, w_hbm,
+    q_hbm, k_hbm, v_hbm, f_hbm, s_hbm, og_hbm, w_hbm,
     qg_ref, kg_ref, vg_ref, fg_ref, sg_ref,
+    q_ref, k_ref, v_ref, f_ref, s_ref, og_ref, in_sem,
     wv, ogb, x, xp, g, gn, a1, b1, a2, b2, mg, filt, part, rsb, red,
     w_sem, og_send, og_recv, fw_send, x_send, x_recv, g_send, g_recv,
     rs_send, rs_recv, ag_send, ag_recv,
@@ -34,6 +35,18 @@
     across_mate = [a + 1 - 2 * lax.rem(a, 2) for a in across]
     order = [tp, mate] + across + across_mate
 
+    def bring(n, source, target):
+        copy = pltpu.make_async_copy(source, target, in_sem.at[n])
+        copy.start()
+        return copy
+
+    k_in = bring(0, k_hbm, k_ref)
+    v_in = bring(1, v_hbm, v_ref)
+    og_in = bring(2, og_hbm, og_ref)
+    f_in = bring(3, f_hbm, f_ref)
+    s_in = bring(4, s_hbm, s_ref)
+    q_in = bring(5, q_hbm, q_ref)
+
     w_copies = []
     for n, slot in enumerate(order):
         copy = pltpu.make_async_copy(
@@ -50,11 +63,15 @@
     def _(d):
         pl.semaphore_signal(barrier, inc=1, device_id=(lax.rem(me + d, n_ctx), tp), device_id_type=MESH)
 
+    k_in.wait()
+    v_in.wait()
+
     @pl.loop(0, tiles)
     def _(i):
         cols = pl.ds(pl.multiple_of(i * LANES, LANES), LANES)
         x[i] = (k_ref[:, cols].astype(jnp.float32) * v_ref[:, cols].astype(jnp.float32)).astype(jnp.bfloat16)
 
+    og_in.wait()
     pl.semaphore_wait(barrier, n_tp - 1 + n_ctx - 1)
 
     def og_copy(p, n, peer):
@@ -85,6 +102,7 @@
     def _():
         x_copy.start()
 
+    f_in.wait()
     row = lax.broadcasted_iota(jnp.int32, (rows, LANES), 0)
     col = lax.broadcasted_iota(jnp.int32, (rows, LANES), 1)
     mirror = jnp.where(lax.rem(row + col, LANES) == 0, 1.0, 0.0).astype(jnp.bfloat16)
@@ -150,6 +168,8 @@
             forward_copy(a, p, n).wait_recv()
             forward_copy(a, p, n).start()
 
+    s_in.wait()
+
     @pl.loop(0, tiles)
     def _(i):
         cols = pl.ds(pl.multiple_of(i * LANES, LANES), LANES)
@@ -165,6 +185,8 @@
             forward_copy(a, p, n).wait_recv()
         w_copies[2 + len(across) + n].wait()
         project(2 + len(across) + n, lambda p, a=a: ogb[a, p], False)
+
+    q_in.wait()
 
     def g_copy(i):
         return pltpu.make_async_remote_copy(
@@ -306,11 +328,21 @@
             ag_copy(d).wait_send()
 
 
+def write_out(*refs):
+    sem = refs[10]
+    copies = [pltpu.make_async_copy(refs[n], refs[5 + n], sem.at[n]) for n in range(5)]
+    for copy in copies:
+        copy.start()
+    for copy in copies:
+        copy.wait()
+
+
 def on_device(n_ctx, n_tp, q, k, v, filters, skip_gain, out_grad, w_out):
     rows, channels = q.shape
     tiles = channels // LANES
     groups = filters.shape[0]
     block = (groups // tiles) + 8
+    anywhere = pl.BlockSpec(memory_space=pl.ANY)
     vmem = pl.BlockSpec(memory_space=pltpu.VMEM)
     bf, fl = jnp.bfloat16, jnp.float32
     dma = pltpu.SemaphoreType.DMA
@@ -325,9 +357,16 @@
             jax.ShapeDtypeStruct(filters.shape, fl),
             jax.ShapeDtypeStruct((1, channels), fl),
         ),
-        in_specs=[vmem] * 6 + [pl.BlockSpec(memory_space=pl.ANY)],
+        in_specs=[anywhere] * 7,
         out_specs=(vmem,) * 5,
         scratch_shapes=[
+            pltpu.VMEM((rows, channels), bf),
+            pltpu.VMEM((rows, channels), bf),
+            pltpu.VMEM((rows, channels), bf),
+            pltpu.VMEM(filters.shape, fl),
+            pltpu.VMEM((1, channels), fl),
+            pltpu.VMEM((rows, channels), bf),
+            dma((6,)),
             pltpu.VMEM((n_tp, channels, channels), bf),
             pltpu.VMEM((n_tp, PIECES, rows, channels // PIECES), bf),
             slab, slab, slab, slab,
@@ -347,13 +386,20 @@
             dma((n_ctx,)), dma((tiles,)),
         ],
         compiler_params=pltpu.CompilerParams(
-            collective_id=0, has_side_effects=True, vmem_limit_bytes=48 * 1024 * 1024
+            collective_id=0, has_side_effects=True, vmem_limit_bytes=56 * 1024 * 1024
         ),
         cost_estimate=pl.CostEstimate(
             flops=2 * rows * channels * channels * n_tp, bytes_accessed=2 * channels * channels * n_tp, transcendentals=0
         ),
     )(q, k, v, filters, skip_gain.reshape(1, channels), out_grad, w_out)
-    return out[:4] + (out[4].reshape(channels),)
+    out = pl.pallas_call(
+        write_out,
+        out_shape=[jax.ShapeDtypeStruct(o.shape, o.dtype) for o in out],
+        in_specs=[anywhere] * 5,
+        out_specs=[anywhere] * 5,
+        scratch_shapes=[dma((5,))],
+    )(*out)
+    return (out[0], out[1], out[2], out[3], out[4].reshape(channels))
 
 
 def solution(mesh):

time: 42 us -> 60.5 us (1.44)
  Pallas kernels: 32.5 us -> 59.7 us
  local copies, waits for them, and re-layouts: 8.55 us -> 0 us
    pallas_call x0 -> x1, Pallas kernels: none -> 26.1 us  [on_device(): pl.pallas_call(write_out, out_shape=[jax.ShapeDtypeStruct(o.shape, o.dtyp...]
    unnamed x17 -> x0, local copies, waits for them, and re-layouts: 8.55 us -> none
    pallas_call x1, Pallas kernels: 32.5 us -> 33.6 us  [on_device(): pl.pallas_call(functools.partial(kernel, n_ctx, n_tp), out_shape=(jax.Sha...]
where the time goes in v2:
time: 60.5 us; the launch traced here: 60.3 us
  Pallas kernels  59.7 us (99%)
  between operations  0.64 us (1%)
    pallas_call x1, Pallas kernels, on_device(): pl.pallas_call(functools.partial(kernel, n_ctx, n_tp), out_shape=(jax.Sha...  33.6 us
    pallas_call x1, Pallas kernels, on_device(): pl.pallas_call(write_out, out_shape=[jax.ShapeDtypeStruct(o.shape, o.dtyp...  26.1 us

profile of v2, /device:TPU:0, one launch (start us, length us, event | category | flops | bytes accessed | tf_op | source)
XLA Modules:
  0.0 60.3 jit_solution(3346738819131182310)
XLA Ops:
  0.6 33.6 %shard_map.110 = (bf16[128,1024]{1,0:T(8,128)(2,1)}, bf16[128,1024]{1,0:T(8,128)(2,1)}, bf16[128,1024]{1,0:T(8,128)(2,1)}, f32[64,128]{1,0:T(8,128)}, f32[1,1024]{1,0:T(1,128)}) custom-call(bf16[128,1024]{1,0:T(8,128)(2,1)} %q_hbm.1, bf16[128,1024]{1,0:T(8,128)(2,1)} %k_hbm.1, bf16[128,1024]{1,0:T(8,128)(2,1)} %v_hbm.1, f32[64,128]{1,0:T(8,128)} %f_hbm.1, ...), custom_call_target="tpu_custom_call" | custom-call | flops 1073741824 | bytes 8388608 | tf_op jit(solution)/shard_map/pallas_call | solution.py:351
  34.2 26.1 %shard_map.111 = (bf16[128,1024]{1,0:T(8,128)(2,1)}, bf16[128,1024]{1,0:T(8,128)(2,1)}, bf16[128,1024]{1,0:T(8,128)(2,1)}, f32[64,128]{1,0:T(8,128)}, f32[1,1024]{1,0:T(1,128)}) custom-call(bf16[128,1024]{1,0:T(8,128)(2,1)} %get-tuple-element.15.refs_0_, bf16[128,1024]{1,0:T(8,128)(2,1)} %get-tuple-element.16.refs_1_, ...), custom_call_target="tpu_custom_call" | custom-call | tf_op jit(solution)/shard_map/pallas_call | solution.py:395

commit v3 on v2

--- a/solution.py
+++ b/solution.py
@@ -329,11 +329,15 @@
 
 
 def write_out(*refs):
-    sem = refs[10]
-    copies = [pltpu.make_async_copy(refs[n], refs[5 + n], sem.at[n]) for n in range(5)]
-    for copy in copies:
+    held, sem = refs[10:15], refs[15]
+    ins = [pltpu.make_async_copy(refs[n], held[n], sem.at[0, n]) for n in range(5)]
+    outs = [pltpu.make_async_copy(held[n], refs[5 + n], sem.at[1, n]) for n in range(5)]
+    for copy in ins:
         copy.start()
-    for copy in copies:
+    for n in range(5):
+        ins[n].wait()
+        outs[n].start()
+    for copy in outs:
         copy.wait()
 
 
@@ -342,7 +346,6 @@
     tiles = channels // LANES
     groups = filters.shape[0]
     block = (groups // tiles) + 8
-    anywhere = pl.BlockSpec(memory_space=pl.ANY)
     vmem = pl.BlockSpec(memory_space=pltpu.VMEM)
     bf, fl = jnp.bfloat16, jnp.float32
     dma = pltpu.SemaphoreType.DMA
@@ -357,7 +360,7 @@
             jax.ShapeDtypeStruct(filters.shape, fl),
             jax.ShapeDtypeStruct((1, channels), fl),
         ),
-        in_specs=[anywhere] * 7,
+        in_specs=[pl.BlockSpec(memory_space=pltpu.HBM)] * 7,
         out_specs=(vmem,) * 5,
         scratch_shapes=[
             pltpu.VMEM((rows, channels), bf),
@@ -395,9 +398,10 @@
     out = pl.pallas_call(
         write_out,
         out_shape=[jax.ShapeDtypeStruct(o.shape, o.dtype) for o in out],
-        in_specs=[anywhere] * 5,
-        out_specs=[anywhere] * 5,
-        scratch_shapes=[dma((5,))],
+        in_specs=[pl.BlockSpec(memory_space=pltpu.HBM)] * 5,
+        out_specs=[pl.BlockSpec(memory_space=pltpu.HBM)] * 5,
+        scratch_shapes=[pltpu.VMEM(o.shape, o.dtype) for o in out] + [dma((2, 5))],
+        compiler_params=pltpu.CompilerParams(vmem_limit_bytes=56 * 1024 * 1024),
     )(*out)
     return (out[0], out[1], out[2], out[3], out[4].reshape(channels))
 

time: 60.5 us -> 36.3 us (0.60)
  Pallas kernels: 59.7 us -> 35.5 us
    pallas_call x1, Pallas kernels: 26.1 us -> 1.92 us  [on_device(): pl.pallas_call(write_out, out_shape=[jax.ShapeDtypeStruct(o.shape, o.dtyp...]
where the time goes in v3:
time: 36.3 us; the launch traced here: 36.1 us
  Pallas kernels  35.5 us (98%)
  between operations  0.64 us (2%)
    pallas_call x1, Pallas kernels, on_device(): pl.pallas_call(functools.partial(kernel, n_ctx, n_tp), out_shape=(jax.Sha...  33.6 us
    pallas_call x1, Pallas kernels, on_device(): pl.pallas_call(write_out, out_shape=[jax.ShapeDtypeStruct(o.shape, o.dtyp...  1.92 us

profile of v3, /device:TPU:0, one launch (start us, length us, event | category | flops | bytes accessed | tf_op | source)
XLA Modules:
  0.0 36.1 jit_solution(2596311013185566376)
XLA Ops:
  0.6 33.6 %shard_map.110 = (bf16[128,1024]{1,0:T(8,128)(2,1)}, bf16[128,1024]{1,0:T(8,128)(2,1)}, bf16[128,1024]{1,0:T(8,128)(2,1)}, f32[64,128]{1,0:T(8,128)}, f32[1,1024]{1,0:T(1,128)}) custom-call(bf16[128,1024]{1,0:T(8,128)(2,1)} %q_hbm.1, bf16[128,1024]{1,0:T(8,128)(2,1)} %k_hbm.1, bf16[128,1024]{1,0:T(8,128)(2,1)} %v_hbm.1, f32[64,128]{1,0:T(8,128)} %f_hbm.1, ...), custom_call_target="tpu_custom_call" | custom-call | flops 1073741824 | bytes 8388608 | tf_op jit(solution)/shard_map/pallas_call | solution.py:354
  34.2 1.9 %shard_map.111 = (bf16[128,1024]{1,0:T(8,128)(2,1)}, bf16[128,1024]{1,0:T(8,128)(2,1)}, bf16[128,1024]{1,0:T(8,128)(2,1)}, f32[64,128]{1,0:T(8,128)}, f32[1,1024]{1,0:T(1,128)}) custom-call(bf16[128,1024]{1,0:T(8,128)(2,1)} %get-tuple-element.15.refs_0_, bf16[128,1024]{1,0:T(8,128)(2,1)} %get-tuple-element.16.refs_1_, ...), custom_call_target="tpu_custom_call" | custom-call | tf_op jit(solution)/shard_map/pallas_call | solution.py:398

commit v4 on v3

--- a/solution.py
+++ b/solution.py
@@ -18,7 +18,7 @@
     q_hbm, k_hbm, v_hbm, f_hbm, s_hbm, og_hbm, w_hbm,
     qg_ref, kg_ref, vg_ref, fg_ref, sg_ref,
     q_ref, k_ref, v_ref, f_ref, s_ref, og_ref, in_sem,
-    wv, ogb, x, xp, g, gn, a1, b1, a2, b2, mg, filt, part, rsb, red,
+    wv, ogb, x, xp, g, gn, a1, b1, a2, b2, mg, part, rsb, red,
     w_sem, og_send, og_recv, fw_send, x_send, x_recv, g_send, g_recv,
     rs_send, rs_recv, ag_send, ag_recv,
 ):
@@ -110,7 +110,7 @@
     def spread(line):
         return pltpu.roll(jnp.broadcast_to(line, (rows, LANES)), 0, 1, stride=1, stride_axis=0)
 
-    @pl.loop(0, tiles)
+    @pl.loop(0, tiles, unroll=4)
     def _(i):
         taps = f_ref[pl.ds(pl.multiple_of(i * per_tile, per_tile), per_tile), :]
         back = jnp.dot(taps.astype(jnp.bfloat16), mirror, preferred_element_type=jnp.float32)
@@ -133,7 +133,7 @@
         return jnp.concatenate([block * m for m in masks], axis=0)
 
     def project(n, block_of, first):
-        @pl.loop(0, tiles // 2)
+        @pl.loop(0, tiles // 2, unroll=4)
         def _(i):
             chans = pl.ds(pl.multiple_of(i * 2 * LANES, 2 * LANES), 2 * LANES)
             total = None
@@ -168,15 +168,6 @@
             forward_copy(a, p, n).wait_recv()
             forward_copy(a, p, n).start()
 
-    s_in.wait()
-
-    @pl.loop(0, tiles)
-    def _(i):
-        cols = pl.ds(pl.multiple_of(i * LANES, LANES), LANES)
-        y = jnp.dot(a1[i], by_group(xp[i]), preferred_element_type=jnp.float32)
-        y += jnp.dot(b1[i], by_group(x[i]), preferred_element_type=jnp.float32)
-        filt[:, cols] = y + s_ref[:, cols] * x[i].astype(jnp.float32)
-
     for n, a in enumerate(across):
         w_copies[2 + n].wait()
         project(2 + n, lambda p, a=a: ogb[a, p], False)
@@ -204,14 +195,12 @@
         def _():
             g_copy(i).start()
 
-        qg_ref[:, cols] = (m * filt[:, cols]).astype(jnp.bfloat16)
-
     flip = jnp.where(row + col == rows - 1, 1.0, 0.0).astype(jnp.bfloat16)
 
     def upside_down(block):
         return jnp.dot(flip, block, preferred_element_type=jnp.float32).astype(jnp.bfloat16)
 
-    @pl.loop(0, tiles)
+    @pl.loop(0, tiles, unroll=4)
     def _(i):
         gt = g[i]
         far = lax.dot_general(by_group(upside_down(xp[i])), gt, NT, preferred_element_type=jnp.float32)
@@ -247,7 +236,17 @@
         def _():
             rs_copy(i).start()
 
-    @pl.loop(0, tiles)
+    s_in.wait()
+
+    @pl.loop(0, tiles, unroll=4)
+    def _(i):
+        cols = pl.ds(pl.multiple_of(i * LANES, LANES), LANES)
+        y = jnp.dot(a1[i], by_group(xp[i]), preferred_element_type=jnp.float32)
+        y += jnp.dot(b1[i], by_group(x[i]), preferred_element_type=jnp.float32)
+        y += s_ref[:, cols] * x[i].astype(jnp.float32)
+        qg_ref[:, cols] = (mg[:, cols] * y).astype(jnp.bfloat16)
+
+    @pl.loop(0, tiles, unroll=4)
     def _(i):
         cols = pl.ds(pl.multiple_of(i * LANES, LANES), LANES)
         z = jnp.dot(b2[i], by_group(g[i]), preferred_element_type=jnp.float32)
@@ -375,7 +374,6 @@
             slab, slab, slab, slab,
             table, table, table, table,
             pltpu.VMEM((rows, channels), fl),
-            pltpu.VMEM((rows, channels), fl),
             pltpu.VMEM((tiles, block, LANES), fl),
             pltpu.VMEM((n_ctx, block, LANES), fl),
             pltpu.VMEM((tiles, block, LANES), fl),

time: 36.3 us -> 32.1 us (0.88)
  Pallas kernels: 35.5 us -> 31.3 us
    pallas_call x1, Pallas kernels: 33.6 us -> 29.4 us  [on_device(): pl.pallas_call(functools.partial(kernel, n_ctx, n_tp), out_shape=(jax.Sha...]
where the time goes in v4:
time: 32.1 us; the launch traced here: 32 us
  Pallas kernels  31.3 us (98%)
  between operations  0.64 us (2%)
    pallas_call x1, Pallas kernels, on_device(): pl.pallas_call(functools.partial(kernel, n_ctx, n_tp), out_shape=(jax.Sha...  29.4 us
    pallas_call x1, Pallas kernels, on_device(): pl.pallas_call(write_out, out_shape=[jax.ShapeDtypeStruct(o.shape, o.dtyp...  1.92 us

profile of v4, /device:TPU:0, one launch (start us, length us, event | category | flops | bytes accessed | tf_op | source)
XLA Modules:
  0.0 32.0 jit_solution(12259737711055438358)
XLA Ops:
  0.6 29.4 %shard_map.110 = (bf16[128,1024]{1,0:T(8,128)(2,1)}, bf16[128,1024]{1,0:T(8,128)(2,1)}, bf16[128,1024]{1,0:T(8,128)(2,1)}, f32[64,128]{1,0:T(8,128)}, f32[1,1024]{1,0:T(1,128)}) custom-call(bf16[128,1024]{1,0:T(8,128)(2,1)} %q_hbm.1, bf16[128,1024]{1,0:T(8,128)(2,1)} %k_hbm.1, bf16[128,1024]{1,0:T(8,128)(2,1)} %v_hbm.1, f32[64,128]{1,0:T(8,128)} %f_hbm.1, ...), custom_call_target="tpu_custom_call" | custom-call | flops 1073741824 | bytes 8388608 | tf_op jit(solution)/shard_map/pallas_call | solution.py:353
  30.0 1.9 %shard_map.111 = (bf16[128,1024]{1,0:T(8,128)(2,1)}, bf16[128,1024]{1,0:T(8,128)(2,1)}, bf16[128,1024]{1,0:T(8,128)(2,1)}, f32[64,128]{1,0:T(8,128)}, f32[1,1024]{1,0:T(1,128)}) custom-call(bf16[128,1024]{1,0:T(8,128)(2,1)} %get-tuple-element.15.refs_0_, bf16[128,1024]{1,0:T(8,128)(2,1)} %get-tuple-element.16.refs_1_, ...), custom_call_target="tpu_custom_call" | custom-call | tf_op jit(solution)/shard_map/pallas_call | solution.py:396

commit v5 on v4

--- a/solution.py
+++ b/solution.py
@@ -107,6 +107,11 @@
     col = lax.broadcasted_iota(jnp.int32, (rows, LANES), 1)
     mirror = jnp.where(lax.rem(row + col, LANES) == 0, 1.0, 0.0).astype(jnp.bfloat16)
 
+    above = jnp.where(col > row, 1.0, 0.0).astype(jnp.bfloat16)
+    not_above = jnp.where(col <= row, 1.0, 0.0).astype(jnp.bfloat16)
+    below = jnp.where(col < row, 1.0, 0.0).astype(jnp.bfloat16)
+    not_below = jnp.where(col >= row, 1.0, 0.0).astype(jnp.bfloat16)
+
     def spread(line):
         return pltpu.roll(jnp.broadcast_to(line, (rows, LANES)), 0, 1, stride=1, stride_axis=0)
 
@@ -116,12 +121,12 @@
         back = jnp.dot(taps.astype(jnp.bfloat16), mirror, preferred_element_type=jnp.float32)
         for j in range(per_tile):
             at = pl.ds(j * LANES, LANES)
-            c1 = spread(back[j : j + 1])
-            a1[i, :, at] = jnp.where(col > row, c1, 0.0).astype(jnp.bfloat16)
-            b1[i, :, at] = jnp.where(col <= row, c1, 0.0).astype(jnp.bfloat16)
-            c2 = spread(taps[j : j + 1])
-            a2[i, :, at] = jnp.where(col < row, c2, 0.0).astype(jnp.bfloat16)
-            b2[i, :, at] = jnp.where(col >= row, c2, 0.0).astype(jnp.bfloat16)
+            c1 = spread(back[j : j + 1]).astype(jnp.bfloat16)
+            a1[i, :, at] = c1 * above
+            b1[i, :, at] = c1 * not_above
+            c2 = spread(taps[j : j + 1]).astype(jnp.bfloat16)
+            a2[i, :, at] = c2 * below
+            b2[i, :, at] = c2 * not_below
 
     lane = lax.broadcasted_iota(jnp.int32, (1, LANES), 1)
     masks = [
@@ -151,22 +156,14 @@
     project(0, lambda p: og_ref[:, pl.ds(p * wide, wide)], True)
 
     for p in range(PIECES):
+        for n, a in enumerate(across):
+            forward_copy(a, p, n).wait_recv()
+            forward_copy(a, p, n).start()
+
+    for p in range(PIECES):
         forward_copy(mate, p, 0).wait_recv()
     w_copies[1].wait()
     project(1, lambda p: ogb[mate, p], False)
-
-    @pl.when(me > 0)
-    def _():
-        x_copy.wait_recv()
-
-    @pl.when(me == 0)
-    def _():
-        xp[...] = jnp.zeros_like(xp)
-
-    for p in range(PIECES):
-        for n, a in enumerate(across):
-            forward_copy(a, p, n).wait_recv()
-            forward_copy(a, p, n).start()
 
     for n, a in enumerate(across):
         w_copies[2 + n].wait()
@@ -199,6 +196,14 @@
 
     def upside_down(block):
         return jnp.dot(flip, block, preferred_element_type=jnp.float32).astype(jnp.bfloat16)
+
+    @pl.when(me > 0)
+    def _():
+        x_copy.wait_recv()
+
+    @pl.when(me == 0)
+    def _():
+        xp[...] = jnp.zeros_like(xp)
 
     @pl.loop(0, tiles, unroll=4)
     def _(i):

time: 32.1 us -> 32 us (level)
  no operation moved by 1% of the time
where the time goes in v5:
time: 32 us; the launch traced here: 31.9 us
  Pallas kernels  31.2 us (98%)
  between operations  0.64 us (2%)
    pallas_call x1, Pallas kernels, on_device(): pl.pallas_call(functools.partial(kernel, n_ctx, n_tp), out_shape=(jax.Sha...  29.3 us
    pallas_call x1, Pallas kernels, on_device(): pl.pallas_call(write_out, out_shape=[jax.ShapeDtypeStruct(o.shape, o.dtyp...  1.92 us

profile of v5, /device:TPU:0, one launch (start us, length us, event | category | flops | bytes accessed | tf_op | source)
XLA Modules:
  0.0 31.9 jit_solution(2733560308004863083)
XLA Ops:
  0.6 29.3 %shard_map.110 = (bf16[128,1024]{1,0:T(8,128)(2,1)}, bf16[128,1024]{1,0:T(8,128)(2,1)}, bf16[128,1024]{1,0:T(8,128)(2,1)}, f32[64,128]{1,0:T(8,128)}, f32[1,1024]{1,0:T(1,128)}) custom-call(bf16[128,1024]{1,0:T(8,128)(2,1)} %q_hbm.1, bf16[128,1024]{1,0:T(8,128)(2,1)} %k_hbm.1, bf16[128,1024]{1,0:T(8,128)(2,1)} %v_hbm.1, f32[64,128]{1,0:T(8,128)} %f_hbm.1, ...), custom_call_target="tpu_custom_call" | custom-call | flops 1073741824 | bytes 8388608 | tf_op jit(solution)/shard_map/pallas_call | solution.py:358
  29.9 1.9 %shard_map.111 = (bf16[128,1024]{1,0:T(8,128)(2,1)}, bf16[128,1024]{1,0:T(8,128)(2,1)}, bf16[128,1024]{1,0:T(8,128)(2,1)}, f32[64,128]{1,0:T(8,128)}, f32[1,1024]{1,0:T(1,128)}) custom-call(bf16[128,1024]{1,0:T(8,128)(2,1)} %get-tuple-element.15.refs_0_, bf16[128,1024]{1,0:T(8,128)(2,1)} %get-tuple-element.16.refs_1_, ...), custom_call_target="tpu_custom_call" | custom-call | tf_op jit(solution)/shard_map/pallas_call | solution.py:401

commit v6 on v4

--- a/solution.py
+++ b/solution.py
@@ -277,16 +277,20 @@
         def _(d):
             ag_copy(d).start()
 
-    @pl.loop(0, tiles)
+    @pl.when(me < n_ctx - 1)
+    def _():
+        @pl.loop(0, tiles)
+        def _(i):
+            g_copy(i).wait_recv()
+
+    @pl.when(me == n_ctx - 1)
+    def _():
+        gn[...] = jnp.zeros_like(gn)
+
+    @pl.loop(0, tiles, unroll=4)
     def _(i):
         cols = pl.ds(pl.multiple_of(i * LANES, LANES), LANES)
-
-        @pl.when(me < n_ctx - 1)
-        def _():
-            g_copy(i).wait_recv()
-            mg[:, cols] += jnp.dot(a2[i], by_group(gn[i]), preferred_element_type=jnp.float32)
-
-        z = mg[:, cols]
+        z = mg[:, cols] + jnp.dot(a2[i], by_group(gn[i]), preferred_element_type=jnp.float32)
         kg_ref[:, cols] = (z * v_ref[:, cols].astype(jnp.float32)).astype(jnp.bfloat16)
         vg_ref[:, cols] = (z * k_ref[:, cols].astype(jnp.float32)).astype(jnp.bfloat16)
 

time: 32.1 us -> 32.1 us (level)
  no operation moved by 1% of the time
where the time goes in v6:
time: 32.1 us; the launch traced here: 32 us
  Pallas kernels  31.3 us (98%)
  between operations  0.64 us (2%)
    pallas_call x1, Pallas kernels, on_device(): pl.pallas_call(functools.partial(kernel, n_ctx, n_tp), out_shape=(jax.Sha...  29.4 us
    pallas_call x1, Pallas kernels, on_device(): pl.pallas_call(write_out, out_shape=[jax.ShapeDtypeStruct(o.shape, o.dtyp...  1.92 us

profile of v6, /device:TPU:0, one launch (start us, length us, event | category | flops | bytes accessed | tf_op | source)
XLA Modules:
  0.0 32.0 jit_solution(14943021492507848801)
XLA Ops:
  0.6 29.4 %shard_map.110 = (bf16[128,1024]{1,0:T(8,128)(2,1)}, bf16[128,1024]{1,0:T(8,128)(2,1)}, bf16[128,1024]{1,0:T(8,128)(2,1)}, f32[64,128]{1,0:T(8,128)}, f32[1,1024]{1,0:T(1,128)}) custom-call(bf16[128,1024]{1,0:T(8,128)(2,1)} %q_hbm.1, bf16[128,1024]{1,0:T(8,128)(2,1)} %k_hbm.1, bf16[128,1024]{1,0:T(8,128)(2,1)} %v_hbm.1, f32[64,128]{1,0:T(8,128)} %f_hbm.1, ...), custom_call_target="tpu_custom_call" | custom-call | flops 1073741824 | bytes 8388608 | tf_op jit(solution)/shard_map/pallas_call | solution.py:357
  30.0 1.9 %shard_map.111 = (bf16[128,1024]{1,0:T(8,128)(2,1)}, bf16[128,1024]{1,0:T(8,128)(2,1)}, bf16[128,1024]{1,0:T(8,128)(2,1)}, f32[64,128]{1,0:T(8,128)}, f32[1,1024]{1,0:T(1,128)}) custom-call(bf16[128,1024]{1,0:T(8,128)(2,1)} %get-tuple-element.15.refs_0_, bf16[128,1024]{1,0:T(8,128)(2,1)} %get-tuple-element.16.refs_1_, ...), custom_call_target="tpu_custom_call" | custom-call | tf_op jit(solution)/shard_map/pallas_call | solution.py:400
